TPU v7x, 32 devices: a whole 2x2x4 slice. The times are simulated.
32 devices in a mesh: groups: 2 (over x), blk: 16 (over z, y, core).
Axes of the slice: x: 2, y: 2, z: 4, core: 2. Of those that a mesh axis runs over, the one named last changes fastest.
Arguments:
- embeddings: float32 [32768, 1024], P(('groups', 'blk')), parts along dimension 0, may hold values from -16 to 16
- cluster_id: int32 [32768], P(('groups', 'blk')), parts along dimension 0, may hold values from 0 to 15, as said below
Outputs:
- nearest: float32 [32768], P(('groups', 'blk')), parts along dimension 0
There are 2 independent parts, one for each index of `groups`. A program takes and returns all parts, laid end to end along the dimension named above; each array names one. Nothing has to cross between parts.
Inputs may be any that keep to these rules, and one draw needn't show every extreme that they name: `cluster_id`: among the rows of one index of blk no cluster appears more than 128 times, and some cluster appears exactly 128 times; every cluster has 128 or more rows in the slab.
All inputs are finite; a program needn't handle non-finite values.
Results may differ from a plain program's by a relative error of at most 0.0003.
Values may be sent and summed in bfloat16 or wider, within the bound.
A program may use at most 64 MiB of HBM per device.

v0:
```python
import jax
import jax.numpy as jnp
from jax import lax
from jax.sharding import PartitionSpec as P


def body(embeddings, cluster_id):
    local_rows, width = embeddings.shape
    owners = lax.axis_size("blk")
    capacity = 2 * local_rows // owners
    total_slots = owners * capacity
    sums = jnp.sum(embeddings * embeddings, axis=1, keepdims=True)
    unit = (embeddings / jnp.sqrt(sums + 1e-06)).astype(jnp.bfloat16)
    one_hot = (cluster_id[:, None] == jnp.arange(owners, dtype=jnp.int32)[None, :]).astype(
        jnp.int32
    )
    earlier = jnp.cumsum(one_hot, axis=0) - one_hot
    row_rank = jnp.sum(earlier * one_hot, axis=1)
    send_slot = cluster_id * capacity + row_rank
    outgoing = jnp.zeros((total_slots, width), jnp.bfloat16).at[send_slot].set(unit)
    out_flags = jnp.zeros((total_slots,), jnp.int32).at[send_slot].set(1)
    arrived, in_flags = (
        lax.all_to_all(
            outgoing.reshape(owners, capacity, width),
            "blk",
            split_axis=0,
            concat_axis=0,
            tiled=True,
        ),
        lax.all_to_all(
            out_flags.reshape(owners, capacity), "blk", split_axis=0, concat_axis=0, tiled=True
        ),
    )
    cluster_rows = arrived.reshape(total_slots, width)
    valid = in_flags.reshape(total_slots) == 1
    scores = lax.dot_general(
        cluster_rows, cluster_rows, (((1,), (1,)), ((), ())), preferred_element_type=jnp.float32
    )
    places = jnp.arange(total_slots, dtype=jnp.int32)
    usable = valid[None, :] & (places[:, None] != places[None, :])
    best_match = jnp.max(jnp.where(usable, scores, jnp.float32(-2.0)), axis=1)
    answers = lax.all_to_all(
        best_match.reshape(owners, capacity), "blk", split_axis=0, concat_axis=0, tiled=True
    )
    return answers.reshape(total_slots)[send_slot]


def solution(mesh):
    in_specs = (P(("groups", "blk"), None), P(("groups", "blk")))
    out_specs = P(("groups", "blk"))
    return jax.shard_map(body, mesh=mesh, in_specs=in_specs, out_specs=out_specs, check_vma=False)
```

profile of v0, /device:TPU:0, one launch (start us, length us, event | category | flops | bytes accessed | tf_op | source)
XLA Modules:
  0.0 165.4 jit_solution(5024997075236536466)
XLA Ops:
  0.0 0.7 fusion.7
  0.7 4.5 %reduce-window.6 = s32[16,8,128]{2,1,0:T(8,128)S(1)} reduce-window(s32[16,8,128]{2,1,0:T(8,128)S(1)} %fusion.7, s32[]{:T(128)} %constant.9.clone.1), window={size=1x1x128 pad=0_0x0_0x127_0}, to_apply=%region_0.0 | reduce-window | flops 2080768 | bytes 131076 | tf_op jit(solution)/shard_map/reduce-window
  5.2 0.1 slice.10
  5.3 0.1 copy.7
  5.4 0.1 copy.8
  5.5 0.1 broadcast_add_fusion
  5.6 0.7 fusion.6
  6.3 0.7 broadcast_clamp_fusion
  7.0 4.9 %scatter_custom_fusion = s32[2048]{0:T(1024)} fusion(s32[1024]{0:T(1024)S(1)} %get-tuple-element.6, s32[1024]{0:T(1024)S(1)} %broadcast.36, s32[]{:T(128)} %constant.9.clone.1), kind=kCustom, calls=%fused_computation.22 | custom fusion | bytes 8196 | tf_op jit(solution)/shard_map/scatter | solution.py:21
  11.9 7.4 %all-to-all-start = ((s32[16,1,128]{2,1,0:T(1,128)}), s32[16,1,128]{2,1,0:T(1,128)S(1)}, u32[]{:S(2)}, u32[]{:S(2)}) async-start(s32[16,1,128]{2,1,0:T(1,128)} %bitcast.3), calls=%async_computation | async-start | bytes 16384 | tf_op jit(solution)/shard_map/all_to_all | solution.py:30
  19.3 2.5 %multiply_reduce_fusion = f32[1024]{0:T(1024)S(1)} fusion(f32[1024,1024]{1,0:T(8,128)} %param.2), kind=kLoop, calls=%fused_computation.7 | loop fusion | flops 2096128 | bytes 4198400 | tf_op jit(solution)/shard_map/reduce_sum | solution.py:12
  21.8 9.2 %scatter_custom_fusion.1 = bf16[2048,1024]{1,0:T(8,128)(2,1)} fusion(s32[1024]{0:T(1024)S(1)} %get-tuple-element.6, f32[1024,1024]{1,0:T(8,128)} %param.2, f32[1024]{0:T(1024)S(1)} %add_sqrt_fusion, bf16[]{:T(256)} %constant.3.clone.1), kind=kCustom, calls=%fused_computation.8 | custom fusion | flops 2097152 | bytes 8392706 | tf_op jit(solution)/shard_map/scatter | solution.py:20
  31.1 0.0 all-to-all-done
  31.1 6.1 %all-to-all-start.1 = ((bf16[16,128,1024]{2,1,0:T(8,128)(2,1)}), bf16[16,128,1024]{2,1,0:T(8,128)(2,1)}, u32[]{:S(2)}, u32[]{:S(2)}) async-start(bf16[16,128,1024]{2,1,0:T(8,128)(2,1)} %bitcast.32), calls=%async_computation.1 | async-start | bytes 8388608 | tf_op jit(solution)/shard_map/all_to_all | solution.py:23
  37.2 77.7 %all-to-all-done.1 = bf16[16,128,1024]{2,1,0:T(8,128)(2,1)} async-done(((bf16[16,128,1024]{2,1,0:T(8,128)(2,1)}), bf16[16,128,1024]{2,1,0:T(8,128)(2,1)}, u32[]{:S(2)}, u32[]{:S(2)}) %all-to-all-start.1) | async-done | bytes 4194336 | tf_op jit(solution)/shard_map/all_to_all | solution.py:23
  114.8 14.1 %select_reduce_fusion = f32[2048]{0:T(1024)S(1)} fusion(pred[2048]{0:T(1024)(128)(4,1)S(1)} %compare_bitcast_fusion, bf16[2048,1024]{1,0:T(8,128)(2,1)} %bitcast.7), kind=kOutput, calls=%fused_computation.3 | convolution fusion | flops 8606709760 | bytes 4204544 | tf_op jit(solution)/shard_map/dot_general | solution.py:36
  129.0 25.8 %all_to_all.23 = f32[16,1,128]{2,1,0:T(1,128)S(1)} all-to-all(f32[16,1,128]{2,1,0:T(1,128)S(1)} %bitcast.37), channel_id=1, replica_groups=mesh['groups'=2,'blk'=16] {'blk'}, dimensions={0} | all-to-all | bytes 16384 | tf_op jit(solution)/shard_map/all_to_all | solution.py:42
  154.8 10.5 %gather_fusion = f32[1024]{0:T(1024)} fusion(f32[2048]{0:T(1024)S(1)} %bitcast.31, s32[1024]{0:T(1024)S(1)} %get-tuple-element.5), kind=kCustom, calls=%fused_computation | custom fusion | bytes 12288 | tf_op jit(solution)/shard_map/gather | solution.py:45
  (5 shorter events, 0.0 us)
Async XLA Ops:
  11.9 19.2 %all-to-all-start = ((s32[16,1,128]{2,1,0:T(1,128)}), s32[16,1,128]{2,1,0:T(1,128)S(1)}, u32[]{:S(2)}, u32[]{:S(2)}) async-start(s32[16,1,128]{2,1,0:T(1,128)} %bitcast.3), calls=%async_computation | async-start | bytes 16384 | tf_op jit(solution)/shard_map/all_to_all | solution.py:30
  31.1 83.7 %all-to-all-start.1 = ((bf16[16,128,1024]{2,1,0:T(8,128)(2,1)}), bf16[16,128,1024]{2,1,0:T(8,128)(2,1)}, u32[]{:S(2)}, u32[]{:S(2)}) async-start(bf16[16,128,1024]{2,1,0:T(8,128)(2,1)} %bitcast.32), calls=%async_computation.1 | async-start | bytes 8388608 | tf_op jit(solution)/shard_map/all_to_all | solution.py:23
where the time goes:
time: 166 us; the launch traced here: 165 us
  waiting for transfers between devices  77.7 us (47%)
  blocking collectives  25.8 us (16%)
  other arithmetic  18.5 us (11%)
  local copies, waits for them, and re-layouts  15.7 us (9%)
  matrix products  14.1 us (8%)
  starting transfers between devices  13.4 us (8%)
    all_to_all x1, waiting for transfers between devices, body(): lax.all_to_all(outgoing.reshape(owners, capacity, width), 'blk', split_ax...  77.7 us
    all_to_all x1, blocking collectives, body(): lax.all_to_all(best_match.reshape(owners, capacity), 'blk', split_axis=0,...  25.8 us
    dot_general x1, matrix products, body(): lax.dot_general(cluster_rows, cluster_rows, (((1,), (1,)), ((), ())), pre...  14.1 us
    gather x1, local copies, waits for them, and re-layouts, body(): return answers.reshape(total_slots)[send_slot]  10.5 us
    scatter x1, other arithmetic, body(): jnp.zeros((total_slots, width), jnp.bfloat16).at[send_slot].set(unit)  9.23 us
    all_to_all x1, starting transfers between devices, body(): lax.all_to_all(out_flags.reshape(owners, capacity), 'blk', split_axis=0,...  7.39 us
    all_to_all x1, starting transfers between devices, body(): lax.all_to_all(outgoing.reshape(owners, capacity, width), 'blk', split_ax...  6.06 us
    scatter x1, local copies, waits for them, and re-layouts, body(): out_flags = jnp.zeros((total_slots,), jnp.int32).at[send_slot].set(1)  4.88 us
  transfers between devices with their start and end apart: 2, of which 1 were waited for; matrix products, arithmetic and copies ran while one was open for 7% of the time, Pallas kernels for 0%

commit v1 on v0

v1 whole, which is shorter than its diff:
```python
import functools

import jax
import jax.numpy as jnp
from jax import lax
from jax.experimental import pallas as pl
from jax.experimental.pallas import tpu as pltpu
from jax.sharding import PartitionSpec as P

LANES = 128
CHUNK = 256
LOW = -4.0
NT = (((1,), (1,)), ((), ()))


def shift_of(place, n):
    i = n - place
    return n // 2 + (i // 2) * (2 * (i % 2) - 1)


def kernel(
    n, cap, emb_ref, id_ref, out_ref, unit, outgoing, arrived, counts_out, counts_in,
    col_bias, best_of, col_best, answers, back,
    send_sem, recv_sem, count_send, count_recv, answer_send, answer_recv,
):
    rows, width = emb_ref.shape
    slots = n * cap
    per_chunk = CHUNK // cap
    me = lax.axis_index("blk")

    barrier = pltpu.get_barrier_semaphore()

    @pl.loop(1, n)
    def _(k):
        pl.semaphore_signal(barrier, inc=1, device_id={"blk": lax.rem(me + k, n)},
                            device_id_type=pl.DeviceIdType.MESH)

    ids = id_ref[...]
    member = lax.broadcasted_iota(jnp.int32, (n, rows), 0) == ids
    one_hot = jnp.where(member, 1.0, 0.0)
    above = (
        lax.broadcasted_iota(jnp.int32, (rows, rows), 0)
        < lax.broadcasted_iota(jnp.int32, (rows, rows), 1)
    )
    earlier = jnp.dot(
        one_hot.astype(jnp.bfloat16),
        jnp.where(above, 1.0, 0.0).astype(jnp.bfloat16),
        preferred_element_type=jnp.float32,
    )
    rank = jnp.sum(earlier * one_hot, axis=0, keepdims=True).astype(jnp.int32)

    @pl.loop(0, rows // LANES)
    def _(t):
        part = pl.ds(pl.multiple_of(t * LANES, LANES), LANES)
        x = emb_ref[part, :]
        total = jnp.sum(x * x, axis=1, keepdims=True)
        unit[part, :] = (x / jnp.sqrt(total + 1e-6)).astype(jnp.bfloat16)

    def target_of(owner):
        return jnp.where(ids == owner, rank, -1)

    def block_of(target):
        pick = lax.broadcasted_iota(jnp.int32, (cap, rows), 0) == target
        pick = jnp.where(pick, 1.0, 0.0).astype(jnp.bfloat16)
        return jnp.dot(pick, unit[...], preferred_element_type=jnp.float32).astype(jnp.bfloat16)

    def count_of(target):
        count = jnp.sum(jnp.where(target >= 0, 1.0, 0.0), axis=1, keepdims=True)
        return jnp.broadcast_to(count, (8, LANES))

    remote = functools.partial(
        pltpu.make_async_remote_copy, device_id_type=pl.DeviceIdType.MESH
    )

    def owner_at(p):
        return lax.rem(me + shift_of(p, n), n)

    def rows_copy(p):
        place = pl.ds(pl.multiple_of(p * cap, cap), cap)
        return remote(outgoing.at[place], arrived.at[place], send_sem.at[p], recv_sem.at[p],
                      device_id={"blk": owner_at(p)})

    def count_copy(p):
        return remote(counts_out.at[p], counts_in.at[p], count_send.at[p], count_recv.at[p],
                      device_id={"blk": owner_at(p)})

    def answer_copy(p):
        return remote(answers.at[p], back.at[p], answer_send.at[p], answer_recv.at[p],
                      device_id={"blk": lax.rem(me - shift_of(p, n) + n, n)})

    pl.semaphore_wait(barrier, n - 1)

    @pl.loop(1, n)
    def _(i):
        p = n - i
        target = target_of(owner_at(p))
        counts_out[p] = count_of(target)
        outgoing[pl.ds(pl.multiple_of(p * cap, cap), cap), :] = block_of(target)
        count_copy(p).start()
        rows_copy(p).start()

    target = target_of(me)
    counts_in[0] = count_of(target)
    arrived[pl.ds(0, cap), :] = block_of(target)

    for j in range(slots // CHUNK):
        for p in range(j * per_chunk, (j + 1) * per_chunk):
            if p > 0:
                count_copy(p).wait_recv()
                rows_copy(p).wait_recv()
            inside = lax.broadcasted_iota(jnp.int32, (cap, LANES), 0).astype(jnp.float32)
            col_bias[pl.ds(p * cap, cap), :] = jnp.where(
                inside < counts_in[p][0:1, :], 0.0, LOW
            )
        lo = j * CHUNK
        new = arrived[pl.ds(lo, CHUNK), :]
        bias = col_bias[pl.ds(lo, CHUNK), :]
        row_bias = bias.T[0:1, :]
        own = lax.dot_general(new, new, NT, preferred_element_type=jnp.float32)
        same = (
            lax.broadcasted_iota(jnp.int32, (CHUNK, CHUNK), 0)
            == lax.broadcasted_iota(jnp.int32, (CHUNK, CHUNK), 1)
        )
        own = jnp.where(same, LOW, own + jnp.concatenate([bias] * (CHUNK // LANES), axis=1))
        col = jnp.max(own, axis=0, keepdims=True)
        if j:
            scores = lax.dot_general(
                arrived[pl.ds(0, lo), :], new, NT, preferred_element_type=jnp.float32
            )
            old_bias = col_bias[pl.ds(0, lo), :]
            keyed = scores + jnp.concatenate([old_bias] * (CHUNK // LANES), axis=1)
            col = jnp.maximum(col, jnp.max(keyed, axis=0, keepdims=True))
            masked = scores + row_bias
            best = best_of[pl.ds(0, lo), :]
            for c in range(CHUNK // LANES):
                best = jnp.maximum(best, masked[:, c * LANES:(c + 1) * LANES])
            best_of[pl.ds(0, lo), :] = best
        best_of[pl.ds(lo, CHUNK), :] = jnp.full((CHUNK, LANES), LOW, jnp.float32)
        col_best[:, pl.ds(lo, CHUNK)] = jnp.broadcast_to(col, (8, CHUNK))

    for j in range(slots // CHUNK):
        lo = j * CHUNK
        best = jnp.max(best_of[pl.ds(lo, CHUNK), :].T, axis=0, keepdims=True)
        best = jnp.maximum(best, col_best[0:1, pl.ds(lo, CHUNK)])
        for q in range(per_chunk):
            p = j * per_chunk + q
            mine = best[:, q * cap:(q + 1) * cap]
            if cap < LANES:
                mine = jnp.concatenate([mine] * (LANES // cap), axis=1)
            mine = jnp.broadcast_to(mine, (8, LANES))
            if p > 0:
                answers[p] = mine
                answer_copy(p).start()
            else:
                back[0] = mine

    @pl.loop(1, n)
    def _(p):
        answer_copy(p).wait_recv()
        rows_copy(p).wait_send()
        count_copy(p).wait_send()
        answer_copy(p).wait_send()

    table = back[:, 0, :]
    spread = jnp.where(lax.broadcasted_iota(jnp.int32, (LANES, rows), 0) == rank, 1.0, 0.0)
    picked = jnp.dot(
        table, spread, precision=lax.Precision.HIGHEST, preferred_element_type=jnp.float32
    )
    i = n - lax.broadcasted_iota(jnp.int32, (n, rows), 0)
    shift = n // 2 + jnp.where((i & 1) == 1, i >> 1, -(i >> 1))
    owner = me + jnp.where(i == n, 0, shift)
    owner = jnp.where(owner >= n, owner - n, owner)
    out_ref[...] = jnp.sum(jnp.where(owner == ids, picked, 0.0), axis=0, keepdims=True)


def body(embeddings, cluster_id):
    rows, width = embeddings.shape
    n = lax.axis_size("blk")
    cap = 2 * rows // n
    slots = n * cap
    tile = (n, 8, LANES)
    nearest = pl.pallas_call(
        functools.partial(kernel, n, cap),
        out_shape=jax.ShapeDtypeStruct((1, rows), jnp.float32),
        in_specs=[pl.BlockSpec(memory_space=pltpu.VMEM)] * 2,
        out_specs=pl.BlockSpec(memory_space=pltpu.VMEM),
        scratch_shapes=[
            pltpu.VMEM((rows, width), jnp.bfloat16),
            pltpu.VMEM((slots, width), jnp.bfloat16),
            pltpu.VMEM((slots, width), jnp.bfloat16),
            pltpu.VMEM(tile, jnp.float32),
            pltpu.VMEM(tile, jnp.float32),
            pltpu.VMEM((slots, LANES), jnp.float32),
            pltpu.VMEM((slots, LANES), jnp.float32),
            pltpu.VMEM((8, slots), jnp.float32),
            pltpu.VMEM(tile, jnp.float32),
            pltpu.VMEM(tile, jnp.float32),
        ] + [pltpu.SemaphoreType.DMA((n,))] * 6,
        compiler_params=pltpu.CompilerParams(
            collective_id=0, has_side_effects=True, vmem_limit_bytes=48 * 2**20
        ),
    )(embeddings, cluster_id.reshape(1, rows))
    return nearest.reshape(rows)


def solution(mesh):
    in_specs = (P(("groups", "blk"), None), P(("groups", "blk")))
    out_specs = P(("groups", "blk"))
    return jax.shard_map(body, mesh=mesh, in_specs=in_specs, out_specs=out_specs, check_vma=False)
```

time: 166 us -> 118 us (0.71)
  Pallas kernels: 0 us -> 115 us
  waiting for transfers between devices: 77.7 us -> 0 us
  blocking collectives: 25.8 us -> 0 us
  other arithmetic: 18.5 us -> 0 us
  matrix products: 14.1 us -> 0 us
  starting transfers between devices: 13.4 us -> 0 us
  local copies, waits for them, and re-layouts: 15.7 us -> 3.47 us
    pallas_call x0 -> x1, Pallas kernels: none -> 115 us  [body(): pl.pallas_call(functools.partial(kernel, n, cap), out_shape=jax.ShapeDtyp...]
    all_to_all x2 -> x0, waiting for transfers between devices: 77.7 us -> none  [the longest x1 77.7 us: body(): lax.all_to_all(outgoing.reshape(owners, capacity, width), 'blk', split_ax...]
    all_to_all x1 -> x0, blocking collectives: 25.8 us -> none  [body(): lax.all_to_all(best_match.reshape(owners, capacity), 'blk', split_axis=0,...]
    dot_general x1 -> x0, matrix products: 14.1 us -> none  [body(): lax.dot_general(cluster_rows, cluster_rows, (((1,), (1,)), ((), ())), pre...]
    all_to_all x2 -> x0, starting transfers between devices: 13.4 us -> none  [the longest x1 7.39 us: body(): lax.all_to_all(out_flags.reshape(owners, capacity), 'blk', split_axis=0,...]
    gather x1 -> x0, local copies, waits for them, and re-layouts: 10.5 us -> none  [body(): return answers.reshape(total_slots)[send_slot]]
    scatter x1 -> x0, other arithmetic: 9.23 us -> none  [body(): jnp.zeros((total_slots, width), jnp.bfloat16).at[send_slot].set(unit)]
    scatter x1 -> x0, local copies, waits for them, and re-layouts: 4.88 us -> none  [body(): out_flags = jnp.zeros((total_slots,), jnp.int32).at[send_slot].set(1)]
  transfers between devices with their start and end apart: 2 -> 0, of which waited for: 1 -> 0; matrix products, arithmetic and copies ran while one was open for 7% -> 0% of each run, Pallas kernels for 0% -> 0%
where the time goes in v1:
time: 118 us
  Pallas kernels  115 us (97%)
  local copies, waits for them, and re-layouts  3.47 us (3%)
    pallas_call x1, Pallas kernels, body(): pl.pallas_call(functools.partial(kernel, n, cap), out_shape=jax.ShapeDtyp...  115 us
    unnamed x5, local copies, waits for them, and re-layouts  3.47 us

profile of v1, /device:TPU:0, one launch (start us, length us, event | category | flops | bytes accessed | tf_op | source)
XLA Modules:
  0.0 118.1 jit_solution(17248453773386858710)
XLA Ops:
  0.0 0.0 copy-start
  0.0 2.2 %copy-done = f32[1024,1024]{1,0:T(8,128)S(1)} copy-done((f32[1024,1024]{1,0:T(8,128)S(1)}, f32[1024,1024]{1,0:T(8,128)}, u32[]{:S(2)}) %copy-start) | copy-done | bytes 4194328
  2.2 0.0 copy-start.1
  2.2 0.7 copy-done.1
  2.9 114.6 %shard_map.28 = f32[1,1024]{1,0:T(1,128)S(1)} custom-call(f32[1024,1024]{1,0:T(8,128)S(1)} %copy-done, s32[1,1024]{1,0:T(1,128)S(1)} %bitcast.3), custom_call_target="tpu_custom_call" | custom-call | tf_op jit(solution)/shard_map/pallas_call | solution.py:182
  117.5 0.6 copy.4
Async XLA Ops:
  0.0 2.2 %copy-start = (f32[1024,1024]{1,0:T(8,128)S(1)}, f32[1024,1024]{1,0:T(8,128)}, u32[]{:S(2)}) copy-start(f32[1024,1024]{1,0:T(8,128)} %emb_ref.1) | copy-start | bytes 12582916
  2.2 0.7 copy-start.1

commit v2 on v0

--- a/solution.py
+++ b/solution.py
@@ -1,10 +1,20 @@
+import functools
+import math
+
 import jax
 import jax.numpy as jnp
 from jax import lax
+from jax.experimental import pallas as pl
+from jax.experimental.pallas import tpu as pltpu
 from jax.sharding import PartitionSpec as P
 
-
-def body(embeddings, cluster_id):
+LANES = 128
+GROUP = 4
+LOW = -4.0
+NT = (((1,), (1,)), ((), ()))
+
+
+def padded_body(embeddings, cluster_id):
     local_rows, width = embeddings.shape
     owners = lax.axis_size("blk")
     capacity = 2 * local_rows // owners
@@ -45,6 +55,342 @@
     return answers.reshape(total_slots)[send_slot]
 
 
+def kernel(
+    n, parts, room, spare, chunk, emb_ref, id_ref, out_ref, over_ref, unit, outgoing, arrived,
+    counts_out, counts_in, spill_out, ids_out, ids_in, col_bias, best_of, col_best, answers, back,
+    flag_out, flag_in,
+    send_sem, recv_sem, count_send, count_recv, answer_send, answer_recv,
+    spill_send, spill_recv, ids_send, ids_recv, flag_send, flag_recv,
+):
+    rows, width = emb_ref.shape
+    sets = n // GROUP
+    total = n * (room + spare)
+    me = lax.axis_index("blk")
+    part = lax.axis_index("groups")
+    my_set, my_place = me // GROUP, lax.rem(me, GROUP)
+    remote = functools.partial(
+        pltpu.make_async_remote_copy, device_id_type=pl.DeviceIdType.MESH
+    )
+
+    def owner_at(p):
+        u, v = p // GROUP, p % GROUP
+        return lax.rem(my_set + u, sets) * GROUP + lax.rem(my_place + v, GROUP)
+
+    def source_at(p):
+        u, v = p // GROUP, p % GROUP
+        return lax.rem(my_set + sets - u, sets) * GROUP + lax.rem(my_place + GROUP - v, GROUP)
+
+    def main_at(p):
+        start = p * room + (p // (n // 2)) * (n * spare)
+        return pl.ds(pl.multiple_of(start, 16), room)
+
+    def spill_at(p):
+        return pl.ds(pl.multiple_of((n // 2) * room + p * spare, 16), spare)
+
+    def rows_copy(p):
+        return remote(
+            outgoing.at[pl.ds(pl.multiple_of(p * room, 16), room)], arrived.at[main_at(p)],
+            send_sem.at[p], recv_sem.at[p], device_id={"blk": owner_at(p)},
+        )
+
+    def count_copy(p):
+        return remote(counts_out.at[p], counts_in.at[p], count_send.at[p], count_recv.at[p],
+                      device_id={"blk": owner_at(p)})
+
+    def answer_copy(p):
+        return remote(answers.at[p], back.at[p], answer_send.at[p], answer_recv.at[p],
+                      device_id={"blk": source_at(p)})
+
+    def spill_copies(u):
+        p = u * GROUP
+        to = {"blk": owner_at(p)}
+        return (
+            remote(ids_out.at[u], ids_in.at[p], ids_send.at[p], ids_recv.at[p], device_id=to),
+            remote(spill_out.at[pl.ds(pl.multiple_of(u * spare, 16), spare)],
+                   arrived.at[spill_at(p)], spill_send.at[p], spill_recv.at[p], device_id=to),
+        )
+
+    def relay_copies(u, v):
+        first, p = u * GROUP, u * GROUP + v
+        to = {"blk": my_set * GROUP + lax.rem(my_place + v, GROUP)}
+        return (
+            remote(ids_in.at[first], ids_in.at[p], ids_send.at[p], ids_recv.at[p], device_id=to),
+            remote(arrived.at[spill_at(first)], arrived.at[spill_at(p)],
+                   spill_send.at[p], spill_recv.at[p], device_id=to),
+        )
+
+    def flag_copy(x):
+        return remote(flag_out, flag_in.at[x], flag_send.at[x], flag_recv.at[x],
+                      device_id={"groups": lax.rem(part + x, parts), "blk": me})
+
+    barrier = pltpu.get_barrier_semaphore()
+
+    @pl.loop(1, n)
+    def _(k):
+        pl.semaphore_signal(barrier, inc=1, device_id={"blk": lax.rem(me + k, n)},
+                            device_id_type=pl.DeviceIdType.MESH)
+
+    @pl.loop(1, parts)
+    def _(x):
+        pl.semaphore_signal(
+            barrier, inc=1, device_id={"groups": lax.rem(part + x, parts), "blk": me},
+            device_id_type=pl.DeviceIdType.MESH,
+        )
+
+    ids = id_ref[...]
+    index = lax.broadcasted_iota(jnp.int32, (n, rows), 0)
+    above = (
+        lax.broadcasted_iota(jnp.int32, (rows, rows), 0)
+        < lax.broadcasted_iota(jnp.int32, (rows, rows), 1)
+    )
+    above = jnp.where(above, 1.0, 0.0).astype(jnp.bfloat16)
+
+    def places(chosen):
+        hot = jnp.where(chosen, 1.0, 0.0)
+        earlier = jnp.dot(hot.astype(jnp.bfloat16), above, preferred_element_type=jnp.float32)
+        return jnp.sum(earlier * hot, axis=0, keepdims=True).astype(jnp.int32)
+
+    rank = places(index == ids)
+    excess = rank >= room
+    in_set = (ids >= index * GROUP) & (ids < index * GROUP + GROUP)
+    spill_rank = places(in_set & excess)
+    over = jnp.max(
+        jnp.where(excess & (spill_rank >= spare), 1.0, 0.0), axis=1, keepdims=True
+    )
+
+    @pl.loop(0, rows // LANES)
+    def _(t):
+        some = pl.ds(pl.multiple_of(t * LANES, LANES), LANES)
+        x = emb_ref[some, :]
+        squares = jnp.sum(x * x, axis=1, keepdims=True)
+        unit[some, :] = (x * (1.0 / jnp.sqrt(squares + 1e-6))).astype(jnp.bfloat16)
+
+    def block_of(target, size):
+        pick = lax.broadcasted_iota(jnp.int32, (size, rows), 0) == target
+        pick = jnp.where(pick, 1.0, 0.0).astype(jnp.bfloat16)
+        return jnp.dot(pick, unit[...], preferred_element_type=jnp.float32).astype(jnp.bfloat16)
+
+    def target_of(owner):
+        return jnp.where(ids == owner, rank, -1)
+
+    def count_of(target):
+        count = jnp.sum(jnp.where(target >= 0, 1.0, 0.0), axis=1, keepdims=True)
+        first = lax.broadcasted_iota(jnp.int32, (8, LANES), 0) == 0
+        return jnp.where(first, count, over)
+
+    def spill_of(u):
+        low = lax.rem(my_set + u, sets) * GROUP
+        target = jnp.where((ids >= low) & (ids < low + GROUP) & excess, spill_rank, -1)
+        pick = lax.broadcasted_iota(jnp.int32, (LANES, rows), 0) == target
+        who = jnp.sum(jnp.where(pick, ids.astype(jnp.float32) + 1.0, 0.0), axis=1, keepdims=True)
+        who = jnp.broadcast_to(who - 1.0, (LANES, LANES)).T[0:8, :]
+        return who, block_of(target, spare)
+
+    pl.semaphore_wait(barrier, n - 1 + parts - 1)
+
+    @pl.loop(1, sets)
+    def _(u):
+        who, block = spill_of(u)
+        ids_out[u] = who
+        spill_out[pl.ds(pl.multiple_of(u * spare, 16), spare), :] = block
+        for copy in spill_copies(u):
+            copy.start()
+
+    who, block = spill_of(0)
+    ids_in[0] = who
+    arrived[spill_at(0), :] = block
+
+    @pl.loop(1, GROUP)
+    def _(v):
+        for copy in relay_copies(0, v):
+            copy.start()
+
+    @pl.loop(1, n)
+    def _(p):
+        target = target_of(owner_at(p))
+        counts_out[p] = count_of(target)
+        outgoing[pl.ds(pl.multiple_of(p * room, 16), room), :] = block_of(target, room)
+        count_copy(p).start()
+        rows_copy(p).start()
+
+    target = target_of(me)
+    counts_in[0] = count_of(target)
+    arrived[main_at(0), :] = block_of(target, room)
+
+    @pl.loop(1, sets)
+    def _(u):
+        for copy in spill_copies(u):
+            copy.wait_recv()
+
+        @pl.loop(1, GROUP)
+        def _(v):
+            for copy in relay_copies(u, v):
+                copy.start()
+
+    flag_out[...] = jnp.zeros((8, LANES), jnp.float32)
+
+    def take_main(p):
+        if p:
+            count_copy(p).wait_recv()
+            rows_copy(p).wait_recv()
+        inside = lax.broadcasted_iota(jnp.int32, (room, LANES), 0).astype(jnp.float32)
+        col_bias[main_at(p), :] = jnp.where(inside < counts_in[p][0:1, :], 0.0, LOW)
+        flag_out[...] = jnp.maximum(flag_out[...], counts_in[p][1:2, :])
+
+    def take_spill(p):
+        if p % GROUP:
+            for copy in relay_copies(p // GROUP, p % GROUP):
+                copy.wait_recv()
+        who = jnp.broadcast_to(ids_in[p][0:1, :], (LANES, LANES)).T[0:spare, :]
+        col_bias[spill_at(p), :] = jnp.where(who == me.astype(jnp.float32), 0.0, LOW)
+
+    order = [(take_main, p, room) for p in range(n // 2)]
+    order += [(take_spill, p, spare) for p in range(n)]
+    order += [(take_main, p, room) for p in range(n // 2, n)]
+    end = 0
+    for lo in range(0, total, chunk):
+        while end < lo + chunk:
+            take, p, size = order.pop(0)
+            take(p)
+            end += size
+        new = arrived[pl.ds(lo, chunk), :]
+        bias = col_bias[pl.ds(lo, chunk), :]
+        row_bias = bias.T[0:1, :]
+        own = lax.dot_general(new, new, NT, preferred_element_type=jnp.float32)
+        same = (
+            lax.broadcasted_iota(jnp.int32, (chunk, chunk), 0)
+            == lax.broadcasted_iota(jnp.int32, (chunk, chunk), 1)
+        )
+        own = jnp.where(same, LOW, own + jnp.concatenate([bias] * (chunk // LANES), axis=1))
+        col = jnp.max(own, axis=0, keepdims=True)
+        if lo:
+            scores = lax.dot_general(
+                arrived[pl.ds(0, lo), :], new, NT, preferred_element_type=jnp.float32
+            )
+            old_bias = col_bias[pl.ds(0, lo), :]
+            keyed = scores + jnp.concatenate([old_bias] * (chunk // LANES), axis=1)
+            col = jnp.maximum(col, jnp.max(keyed, axis=0, keepdims=True))
+            masked = scores + row_bias
+            best = best_of[pl.ds(0, lo), :]
+            for c in range(chunk // LANES):
+                best = jnp.maximum(best, masked[:, c * LANES:(c + 1) * LANES])
+            best_of[pl.ds(0, lo), :] = best
+        best_of[pl.ds(lo, chunk), :] = jnp.full((chunk, LANES), LOW, jnp.float32)
+        col_best[:, pl.ds(lo, chunk)] = jnp.broadcast_to(col, (8, chunk))
+
+    @pl.loop(1, parts)
+    def _(x):
+        flag_copy(x).start()
+
+    def best_at(lo):
+        best = jnp.max(best_of[pl.ds(lo, chunk), :].T, axis=0, keepdims=True)
+        return jnp.maximum(best, col_best[0:1, pl.ds(lo, chunk)])
+
+    found = jnp.concatenate([best_at(lo) for lo in range(0, total, chunk)], axis=1)
+
+    def lanes_of(start, size):
+        filler = jnp.zeros((1, LANES - size), jnp.float32)
+        return jnp.concatenate([found[:, start:start + size], filler], axis=1)
+
+    first = lax.broadcasted_iota(jnp.int32, (8, LANES), 0) == 0
+    for p in range(n):
+        main = lanes_of(p * room + (p // (n // 2)) * (n * spare), room)
+        spill = lanes_of((n // 2) * room + p * spare, spare)
+        mine = jnp.where(first, main, spill)
+        if p:
+            answers[p] = mine
+            answer_copy(p).start()
+        else:
+            back[0] = mine
+
+    @pl.loop(1, parts)
+    def _(x):
+        flag_copy(x).wait_recv()
+        flag_copy(x).wait_send()
+
+    every = flag_out[...]
+    for x in range(1, parts):
+        every = jnp.maximum(every, flag_in[x])
+    over_ref[...] = every
+
+    @pl.loop(1, n)
+    def _(p):
+        answer_copy(p).wait_recv()
+        rows_copy(p).wait_send()
+        count_copy(p).wait_send()
+        answer_copy(p).wait_send()
+
+    @pl.loop(1, sets)
+    def _(u):
+        for copy in spill_copies(u):
+            copy.wait_send()
+
+    @pl.loop(0, sets)
+    def _(u):
+        @pl.loop(1, GROUP)
+        def _(v):
+            for copy in relay_copies(u, v):
+                copy.wait_send()
+
+    table = jnp.concatenate([back[:, 0, :], back[:, 1, :]], axis=1)
+    where = jnp.where(excess, LANES + spill_rank, rank)
+    spread = lax.broadcasted_iota(jnp.int32, (2 * LANES, rows), 0) == where
+    picked = jnp.dot(
+        table, jnp.where(spread, 1.0, 0.0), precision=lax.Precision.HIGHEST,
+        preferred_element_type=jnp.float32,
+    )
+    shift = GROUP.bit_length() - 1
+    owner_set = my_set + (index >> shift)
+    owner_set = jnp.where(owner_set >= sets, owner_set - sets, owner_set)
+    owner = owner_set * GROUP + ((my_place + (index & (GROUP - 1))) & (GROUP - 1))
+    out_ref[...] = jnp.sum(jnp.where(owner == ids, picked, 0.0), axis=0, keepdims=True)
+
+
+def body(embeddings, cluster_id):
+    rows, width = embeddings.shape
+    n = lax.axis_size("blk")
+    parts = lax.axis_size("groups")
+    cap = 2 * rows // n
+    room = cap * 3 // 4 // 16 * 16
+    spare = -(-cap * 3 // 8 // 16) * 16
+    chunk = math.lcm(room, spare, LANES)
+    chunk = chunk if chunk > LANES else 2 * chunk
+    total = n * (room + spare)
+    tile = (8, LANES)
+    bf16, f32 = jnp.bfloat16, jnp.float32
+    nearest, over = pl.pallas_call(
+        functools.partial(kernel, n, parts, room, spare, chunk),
+        out_shape=(jax.ShapeDtypeStruct((1, rows), f32), jax.ShapeDtypeStruct(tile, f32)),
+        in_specs=[pl.BlockSpec(memory_space=pltpu.VMEM)] * 2,
+        out_specs=[pl.BlockSpec(memory_space=pltpu.VMEM)] * 2,
+        scratch_shapes=[
+            pltpu.VMEM((rows, width), bf16),
+            pltpu.VMEM((n * room, width), bf16),
+            pltpu.VMEM((total, width), bf16),
+            pltpu.VMEM((n, *tile), f32),
+            pltpu.VMEM((n, *tile), f32),
+            pltpu.VMEM((n // GROUP * spare, width), bf16),
+            pltpu.VMEM((n // GROUP, *tile), f32),
+            pltpu.VMEM((n, *tile), f32),
+            pltpu.VMEM((total, LANES), f32),
+            pltpu.VMEM((total, LANES), f32),
+            pltpu.VMEM((8, total), f32),
+            pltpu.VMEM((n, *tile), f32),
+            pltpu.VMEM((n, *tile), f32),
+            pltpu.VMEM(tile, f32),
+            pltpu.VMEM((parts, *tile), f32),
+        ] + [pltpu.SemaphoreType.DMA((n,))] * 10 + [pltpu.SemaphoreType.DMA((parts,))] * 2,
+        compiler_params=pltpu.CompilerParams(
+            collective_id=0, has_side_effects=True, vmem_limit_bytes=48 * 2**20
+        ),
+    )(embeddings, cluster_id.reshape(1, rows))
+    return lax.cond(
+        over[0, 0] > 0.0,
+        lambda: padded_body(embeddings, cluster_id),
+        lambda: nearest.reshape(rows),
+    )
+
+
 def solution(mesh):
     in_specs = (P(("groups", "blk"), None), P(("groups", "blk")))
     out_specs = P(("groups", "blk"))

time: 166 us -> 103 us (0.62)
  Pallas kernels: 0 us -> 101 us
  waiting for transfers between devices: 77.7 us -> 0 us
  blocking collectives: 25.8 us -> 0 us
  other arithmetic: 18.5 us -> 0 us
  local copies, waits for them, and re-layouts: 15.7 us -> 1.11 us
  matrix products: 14.1 us -> 0 us
  starting transfers between devices: 13.4 us -> 0 us
    pallas_call x0 -> x1, Pallas kernels: none -> 101 us  [body(): pl.pallas_call(functools.partial(kernel, n, parts, room, spare, chunk), o...]
    all_to_all x2 -> x0, waiting for transfers between devices: 77.7 us -> none  [the longest x1 77.7 us: body(): lax.all_to_all(outgoing.reshape(owners, capacity, width), 'blk', split_ax...]
    all_to_all x1 -> x0, blocking collectives: 25.8 us -> none  [body(): lax.all_to_all(best_match.reshape(owners, capacity), 'blk', split_axis=0,...]
    dot_general x1 -> x0, matrix products: 14.1 us -> none  [body(): lax.dot_general(cluster_rows, cluster_rows, (((1,), (1,)), ((), ())), pre...]
    all_to_all x2 -> x0, starting transfers between devices: 13.4 us -> none  [the longest x1 7.39 us: body(): lax.all_to_all(out_flags.reshape(owners, capacity), 'blk', split_axis=0,...]
    gather x1 -> x0, local copies, waits for them, and re-layouts: 10.5 us -> none  [body(): return answers.reshape(total_slots)[send_slot]]
    scatter x1 -> x0, other arithmetic: 9.23 us -> none  [body(): jnp.zeros((total_slots, width), jnp.bfloat16).at[send_slot].set(unit)]
    scatter x1 -> x0, local copies, waits for them, and re-layouts: 4.88 us -> none  [body(): out_flags = jnp.zeros((total_slots,), jnp.int32).at[send_slot].set(1)]
  transfers between devices with their start and end apart: 2 -> 0, of which waited for: 1 -> 0; matrix products, arithmetic and copies ran while one was open for 7% -> 0% of each run, Pallas kernels for 0% -> 0%
where the time goes in v2:
time: 103 us
  Pallas kernels  101 us (98%)
  local copies, waits for them, and re-layouts  1.11 us (1%)
    pallas_call x1, Pallas kernels, body(): pl.pallas_call(functools.partial(kernel, n, parts, room, spare, chunk), o...  101 us

profile of v2, /device:TPU:0, one launch (start us, length us, event | category | flops | bytes accessed | tf_op | source)
XLA Modules:
  0.0 102.7 jit_solution(13652225428221288872)
XLA Ops:
  0.0 0.0 copy-start
  0.0 100.7 %shard_map.30 = (f32[1,1024]{1,0:T(1,128)S(1)}, f32[8,128]{1,0:T(8,128)S(1)}) custom-call(f32[1024,1024]{1,0:T(8,128)} %emb_ref.1, s32[1,1024]{1,0:T(1,128)} %bitcast.37), custom_call_target="tpu_custom_call" | custom-call | tf_op jit(solution)/shard_map/pallas_call | solution.py:361
  100.7 0.5 slice.9
  101.9 0.0 copy-done
  101.9 0.2 conditional.1
  102.1 0.6 copy.17
Async XLA Ops:
  0.0 101.9 %copy-start = (s32[1024]{0:T(1024)S(1)}, s32[1024]{0:T(1024)}, u32[]{:S(2)}) copy-start(s32[1024]{0:T(1024)} %param.5) | copy-start | bytes 12292

commit v3 on v2

--- a/solution.py
+++ b/solution.py
@@ -1,5 +1,4 @@
 import functools
-import math
 
 import jax
 import jax.numpy as jnp
@@ -10,6 +9,7 @@
 
 LANES = 128
 GROUP = 4
+CHUNK = 256
 LOW = -4.0
 NT = (((1,), (1,)), ((), ()))
 
@@ -311,7 +311,7 @@
     every = flag_out[...]
     for x in range(1, parts):
         every = jnp.maximum(every, flag_in[x])
-    over_ref[...] = every
+    over_ref[0] = jnp.max(every)
 
     @pl.loop(1, n)
     def _(p):
@@ -351,18 +351,15 @@
     n = lax.axis_size("blk")
     parts = lax.axis_size("groups")
     cap = 2 * rows // n
-    room = cap * 3 // 4 // 16 * 16
-    spare = -(-cap * 3 // 8 // 16) * 16
-    chunk = math.lcm(room, spare, LANES)
-    chunk = chunk if chunk > LANES else 2 * chunk
+    room, spare = cap * 5 // 8 // 16 * 16, cap * 3 // 4 // 16 * 16
     total = n * (room + spare)
     tile = (8, LANES)
     bf16, f32 = jnp.bfloat16, jnp.float32
     nearest, over = pl.pallas_call(
-        functools.partial(kernel, n, parts, room, spare, chunk),
-        out_shape=(jax.ShapeDtypeStruct((1, rows), f32), jax.ShapeDtypeStruct(tile, f32)),
+        functools.partial(kernel, n, parts, room, spare, CHUNK),
+        out_shape=(jax.ShapeDtypeStruct((1, rows), f32), jax.ShapeDtypeStruct((1,), f32)),
         in_specs=[pl.BlockSpec(memory_space=pltpu.VMEM)] * 2,
-        out_specs=[pl.BlockSpec(memory_space=pltpu.VMEM)] * 2,
+        out_specs=[pl.BlockSpec(memory_space=pltpu.VMEM), pl.BlockSpec(memory_space=pltpu.SMEM)],
         scratch_shapes=[
             pltpu.VMEM((rows, width), bf16),
             pltpu.VMEM((n * room, width), bf16),
@@ -385,7 +382,7 @@
         ),
     )(embeddings, cluster_id.reshape(1, rows))
     return lax.cond(
-        over[0, 0] > 0.0,
+        over[0] > 0.0,
         lambda: padded_body(embeddings, cluster_id),
         lambda: nearest.reshape(rows),
     )

time: 103 us -> 100 us (0.971)
  Pallas kernels: 101 us -> 99 us
    pallas_call x1, Pallas kernels: 101 us -> 99 us  [body(): pl.pallas_call(functools.partial(kernel, n, parts, room, spare, CHUNK), o...]
where the time goes in v3:
time: 100 us
  Pallas kernels  99 us (99%)
    pallas_call x1, Pallas kernels, body(): pl.pallas_call(functools.partial(kernel, n, parts, room, spare, CHUNK), o...  99 us

profile of v3, /device:TPU:0, one launch (start us, length us, event | category | flops | bytes accessed | tf_op | source)
XLA Modules:
  0.0 100.3 jit_solution(128103663258065459)
XLA Ops:
  0.0 0.0 copy-start
  0.0 99.0 %shard_map.30 = (f32[1,1024]{1,0:T(1,128)S(1)}, f32[1]{0:T(128)}) custom-call(f32[1024,1024]{1,0:T(8,128)} %emb_ref.1, s32[1,1024]{1,0:T(1,128)} %bitcast.37), custom_call_target="tpu_custom_call" | custom-call | tf_op jit(solution)/shard_map/pallas_call | solution.py:358
  99.7 0.0 copy-done
  99.7 0.6 copy.17
  (1 shorter events, 0.0 us)
Async XLA Ops:
  0.0 99.7 %copy-start = (s32[1024]{0:T(1024)S(1)}, s32[1024]{0:T(1024)}, u32[]{:S(2)}) copy-start(s32[1024]{0:T(1024)} %param.5) | copy-start | bytes 12292
